TPU v7x, 32 devices: a whole 2x2x4 slice. The times are simulated.
32 devices in a mesh: batch: 4 (over y, x), seq: 8 (over z, core).
Axes of the slice: x: 2, y: 2, z: 4, core: 2. Of those that a mesh axis runs over, the one named last changes fastest.
Arguments:
- queries: bfloat16 [4, 2048, 1024], P('batch', 'seq'), may hold values from -6 to 6
- key_states: bfloat16 [4, 2048, 1024], P('batch', 'seq'), may hold values from -6 to 6
- value_states: bfloat16 [4, 2048, 1024], P('batch', 'seq'), may hold values from -6 to 6
- out_grad: bfloat16 [4, 2048, 1024], P('batch', 'seq'), may hold values from -6 to 6
- memory: float32 [1024, 1024], replicated, may hold values from -6 to 6
- near_device: int32 [16, 4], replicated, may hold values from 0 to 7, all different within a row; in each aligned block of 2 rows (0 to 1, 2 to 3, ...) no two rows name the same one
- near_slot: int32 [16, 4], replicated, may hold values from 0 to 1
- near_count: int32 [16], replicated, may hold values from 1 to 4, 40 in all
- writer_block: int32 [1024], replicated, may hold values from 0 to 15, as said below
Outputs:
- attended: bfloat16 [4, 2048, 1024], P('batch', 'seq')
- query_grad: bfloat16 [4, 2048, 1024], P('batch', 'seq')
- key_grad: bfloat16 [4, 2048, 1024], P('batch', 'seq')
- value_grad: bfloat16 [4, 2048, 1024], P('batch', 'seq')
- memory_grad: float32 [1024, 1024], P('seq')
Inputs may be any that keep to these rules, and one draw needn't show every extreme that they name: Row n of near_device belongs to block n; one row names different indices; the rows of the 2 blocks of one index of seq name no index more than 1 times. writer_block[r] // 2 == r // 128: a memory row is written by a block of the index of seq that holds the row.
All inputs are finite; a program needn't handle non-finite values.
Results may differ from a plain program's by a relative error of at most 0.025.
Values may be sent and summed in bfloat16 or wider, within the bound.
A program may use at most 192 MiB of HBM per device.

v0:
```python
import math

import jax
import jax.numpy as jnp
from jax import lax
from jax.sharding import PartitionSpec as P

HEADS = 8
HD = 128
BLK = 128
MEM = 1024


def route_tables(near_device, near_slot, seq_devices):
    target = near_device.reshape(seq_devices, -1)
    source_slot = near_slot.reshape(seq_devices, -1)
    position = jnp.arange(target.shape[1])
    earlier = position[None, :] < position[:, None]
    matching = target[:, :, None] == target[:, None, :]
    arrival = jnp.sum(jnp.logical_and(matching, earlier[None, :, :]), axis=2)
    return (target, source_slot, arrival)


def shards(
    queries,
    key_states,
    value_states,
    out_grad,
    memory,
    near_device,
    near_slot,
    near_count,
    writer_block,
):
    seq_devices = lax.axis_size("seq")
    my_index = lax.axis_index("seq")
    tokens = queries.shape[1]
    row_width = queries.shape[2]
    near_width = near_device.shape[1]
    local_blocks = tokens // BLK
    entries = local_blocks * near_width
    capacity = (entries + seq_devices - 1) // seq_devices
    rows_dev = MEM // seq_devices
    key_scaling_factor = 1.0 / math.sqrt(HD)
    block_scale = 1.0 / math.sqrt(BLK)
    value_blocks = value_states[0].reshape(local_blocks, BLK, row_width)
    key_blocks = key_states[0].reshape(local_blocks, BLK, row_width)
    value_sums = jnp.sum(value_blocks, axis=1, dtype=jnp.float32)
    my_writers = (
        lax.dynamic_slice_in_dim(writer_block, my_index * rows_dev, rows_dev, 0)
        - my_index * local_blocks
    )
    mine = lax.dynamic_slice_in_dim(memory, my_index * rows_dev, rows_dev, 0)
    written = (mine + jnp.take(value_sums, my_writers, axis=0) * block_scale).astype(jnp.bfloat16)
    memory_keys = lax.all_gather(written, "seq", axis=0, tiled=True)
    target, source_slot, arrival = route_tables(near_device, near_slot, seq_devices)
    my_target = lax.dynamic_index_in_dim(target, my_index, 0, keepdims=False)
    my_arrival = lax.dynamic_index_in_dim(arrival, my_index, 0, keepdims=False)
    flat_place = my_target * capacity + my_arrival
    entry_slot = (flat_place[:, None] == jnp.arange(seq_devices * capacity)[None, :]).astype(
        jnp.bfloat16
    )
    toward_me = (target == my_index).astype(jnp.float32)
    arrival_hot = (arrival[:, :, None] == jnp.arange(capacity)[None, None, :]).astype(jnp.float32)
    slot_hot = (source_slot[:, :, None] == jnp.arange(local_blocks)[None, None, :]).astype(
        jnp.float32
    )
    select = jnp.einsum("de,des,del->dsl", toward_me, arrival_hot, slot_hot).astype(jnp.bfloat16)
    send_keys = jnp.einsum(
        "dsl,ltw->dstw", select, key_blocks, preferred_element_type=jnp.float32
    ).astype(jnp.bfloat16)
    send_values = jnp.einsum(
        "dsl,ltw->dstw", select, value_blocks, preferred_element_type=jnp.float32
    ).astype(jnp.bfloat16)
    got_keys, got_values = (
        lax.all_to_all(send_keys, "seq", split_axis=0, concat_axis=0, tiled=True),
        lax.all_to_all(send_values, "seq", split_axis=0, concat_axis=0, tiled=True),
    )
    flat_keys = got_keys.reshape(seq_devices * capacity, BLK, row_width)
    flat_values = got_values.reshape(seq_devices * capacity, BLK, row_width)
    neighbour_key_rows = jnp.einsum(
        "ef,ftw->etw", entry_slot, flat_keys, preferred_element_type=jnp.float32
    ).astype(jnp.bfloat16)
    neighbour_value_rows = jnp.einsum(
        "ef,ftw->etw", entry_slot, flat_values, preferred_element_type=jnp.float32
    ).astype(jnp.bfloat16)
    neighbour_key_rows = neighbour_key_rows.reshape(local_blocks, near_width * BLK, HEADS, HD)
    neighbour_value_rows = neighbour_value_rows.reshape(local_blocks, near_width * BLK, HEADS, HD)
    my_count = lax.dynamic_slice_in_dim(near_count, my_index * local_blocks, local_blocks, 0)
    live_keys = jnp.arange(near_width * BLK)[None, :] // BLK < my_count[:, None]
    query_head_states = queries[0].reshape(local_blocks, BLK, HEADS, HD)
    head_output_gradient = out_grad[0].reshape(local_blocks, BLK, HEADS, HD)
    memory_head_states = memory_keys.reshape(MEM, HEADS, HD)
    memory_score_logits = (
        jnp.einsum(
            "xswr,gwr->xwsg",
            query_head_states,
            memory_head_states,
            preferred_element_type=jnp.float32,
        )
        * key_scaling_factor
    )
    score_near = (
        jnp.einsum(
            "cqhd,ckhd->chqk",
            query_head_states,
            neighbour_key_rows,
            preferred_element_type=jnp.float32,
        )
        * key_scaling_factor
    )
    score_near = jnp.where(live_keys[:, None, None, :], score_near, -jnp.inf)
    row_max = jnp.maximum(jnp.max(memory_score_logits, axis=-1), jnp.max(score_near, axis=-1))
    exp_mem = jnp.exp(memory_score_logits - row_max[..., None])
    exp_near = jnp.exp(score_near - row_max[..., None])
    row_total = jnp.sum(exp_mem, axis=-1) + jnp.sum(exp_near, axis=-1)
    prob_mem = exp_mem / row_total[..., None]
    prob_near = exp_near / row_total[..., None]
    memory_attention_weight = prob_mem.astype(jnp.bfloat16)
    neighbour_attention_weight = prob_near.astype(jnp.bfloat16)
    head_attended_output = (
        jnp.einsum(
            "vjpe,eji->vpji",
            memory_attention_weight,
            memory_head_states,
            preferred_element_type=jnp.float32,
        )
        + jnp.einsum(
            "chqk,ckhd->cqhd",
            neighbour_attention_weight,
            neighbour_value_rows,
            preferred_element_type=jnp.float32,
        )
    ).astype(jnp.bfloat16)
    grad_dot = jnp.einsum(
        "cqhd,cqhd->chq",
        head_output_gradient,
        head_attended_output,
        preferred_element_type=jnp.float32,
    )
    memory_probability_gradient = jnp.einsum(
        "xswr,gwr->xwsg",
        head_output_gradient,
        memory_head_states,
        preferred_element_type=jnp.float32,
    )
    dprob_near = jnp.einsum(
        "cqhd,ckhd->chqk",
        head_output_gradient,
        neighbour_value_rows,
        preferred_element_type=jnp.float32,
    )
    memory_score_gradient = (prob_mem * (memory_probability_gradient - grad_dot[..., None])).astype(
        jnp.bfloat16
    )
    neighbour_score_gradient = (prob_near * (dprob_near - grad_dot[..., None])).astype(jnp.bfloat16)
    query_portion = (
        jnp.einsum(
            "vjpe,eji->vpji",
            memory_score_gradient,
            memory_head_states,
            preferred_element_type=jnp.float32,
        )
        + jnp.einsum(
            "chqk,ckhd->cqhd",
            neighbour_score_gradient,
            neighbour_key_rows,
            preferred_element_type=jnp.float32,
        )
    ) * key_scaling_factor
    key_part = (
        jnp.einsum(
            "chqk,cqhd->ckhd",
            neighbour_score_gradient,
            query_head_states,
            preferred_element_type=jnp.float32,
        )
        * key_scaling_factor
    ).astype(jnp.bfloat16)
    value_part = jnp.einsum(
        "chqk,cqhd->ckhd",
        neighbour_attention_weight,
        head_output_gradient,
        preferred_element_type=jnp.float32,
    ).astype(jnp.bfloat16)
    key_part = key_part.reshape(entries, BLK, row_width)
    value_part = value_part.reshape(entries, BLK, row_width)
    back_keys = jnp.einsum(
        "ef,etw->ftw", entry_slot, key_part, preferred_element_type=jnp.float32
    ).astype(jnp.bfloat16)
    back_values = jnp.einsum(
        "ef,etw->ftw", entry_slot, value_part, preferred_element_type=jnp.float32
    ).astype(jnp.bfloat16)
    back_keys = back_keys.reshape(seq_devices, capacity, BLK, row_width)
    back_values = back_values.reshape(seq_devices, capacity, BLK, row_width)
    slot_keys_grad, slot_values_grad = (
        lax.all_to_all(back_keys, "seq", split_axis=0, concat_axis=0, tiled=True),
        lax.all_to_all(back_values, "seq", split_axis=0, concat_axis=0, tiled=True),
    )
    key_sum = jnp.einsum(
        "dsl,dstw->ltw", select, slot_keys_grad, preferred_element_type=jnp.float32
    )
    value_sum = jnp.einsum(
        "dsl,dstw->ltw", select, slot_values_grad, preferred_element_type=jnp.float32
    )
    term = (
        jnp.einsum(
            "irey,ierk->yrk",
            memory_score_gradient,
            query_head_states,
            preferred_element_type=jnp.float32,
        )
        * key_scaling_factor
    )
    term = term + jnp.einsum(
        "irey,ierk->yrk",
        memory_attention_weight,
        head_output_gradient,
        preferred_element_type=jnp.float32,
    )
    row_grads = lax.psum_scatter(
        term.reshape(lax.axis_size("seq") * rows_dev, row_width).astype(jnp.bfloat16),
        "seq",
        scatter_dimension=0,
        tiled=True,
    ).astype(jnp.float32)
    writer_match = (my_writers[:, None] == jnp.arange(local_blocks)[None, :])[:, :, None]
    spread = jnp.sum(jnp.where(writer_match, row_grads[:, None, :], 0.0), axis=0) * block_scale
    memory_grad = lax.psum(row_grads.astype(jnp.bfloat16), "batch").astype(jnp.float32)
    attended = head_attended_output.reshape(1, tokens, row_width)
    query_grad = query_portion.astype(jnp.bfloat16).reshape(1, tokens, row_width)
    key_grad = key_sum.astype(jnp.bfloat16).reshape(1, tokens, row_width)
    value_grad = (value_sum + spread[:, None, :]).astype(jnp.bfloat16).reshape(1, tokens, row_width)
    return (attended, query_grad, key_grad, value_grad, memory_grad)


def solution(mesh):
    placed = (
        P("batch", "seq", None),
        P("batch", "seq", None),
        P("batch", "seq", None),
        P("batch", "seq", None),
        P(),
        P(),
        P(),
        P(),
        P(),
    )
    return jax.shard_map(
        shards,
        mesh=mesh,
        in_specs=placed,
        out_specs=(
            P("batch", "seq", None),
            P("batch", "seq", None),
            P("batch", "seq", None),
            P("batch", "seq", None),
            P("seq", None),
        ),
        check_vma=False,
    )
```

profile of v0, /device:TPU:0, one launch (start us, length us, event | category | flops | bytes accessed | tf_op | source)
XLA Modules:
  0.0 312.8 jit_solution(4679202521501033596)
XLA Ops:
  13.0 6.3 %all-to-all-start = ((bf16[8,1,128,1024]{3,2,1,0:T(8,128)(2,1)}), bf16[8,1,128,1024]{3,2,1,0:T(8,128)(2,1)}, u32[]{:S(2)}, u32[]{:S(2)}) async-start(bf16[8,1,128,1024]{3,2,1,0:T(8,128)(2,1)} %copy.244), calls=%async_computation | async-start | bytes 4194304 | tf_op jit(solution)/shard_map/all_to_all | solution.py:76
  26.5 58.8 %all-to-all-done = bf16[8,1,128,1024]{3,2,1,0:T(8,128)(2,1)} async-done(((bf16[8,1,128,1024]{3,2,1,0:T(8,128)(2,1)}), bf16[8,1,128,1024]{3,2,1,0:T(8,128)(2,1)}, u32[]{:S(2)}, u32[]{:S(2)}) %all-to-all-start) | async-done | bytes 2097184 | tf_op jit(solution)/shard_map/all_to_all | solution.py:76
  85.4 4.5 %all-to-all-start.1 = ((bf16[8,1,128,1024]{3,2,1,0:T(8,128)(2,1)}), bf16[8,1,128,1024]{3,2,1,0:T(8,128)(2,1)}, u32[]{:S(2)}, u32[]{:S(2)}) async-start(bf16[8,1,128,1024]{3,2,1,0:T(8,128)(2,1)} %copy.256), calls=%async_computation.1 | async-start | bytes 4194304 | tf_op jit(solution)/shard_map/all_to_all | solution.py:77
  91.8 2.9 fusion.42
  97.9 2.9 copy.238
  110.2 28.8 %all-to-all-done.1 = bf16[8,1,128,1024]{3,2,1,0:T(8,128)(2,1)} async-done(((bf16[8,1,128,1024]{3,2,1,0:T(8,128)(2,1)}), bf16[8,1,128,1024]{3,2,1,0:T(8,128)(2,1)}, u32[]{:S(2)}, u32[]{:S(2)}) %all-to-all-start.1) | async-done | bytes 2097184 | tf_op jit(solution)/shard_map/all_to_all | solution.py:77
  138.9 3.1 fusion.45
  146.2 3.0 bitcast_convert_fusion
  153.5 4.6 %fusion.6 = bf16[2,8,128,512]{2,3,1,0:T(8,128)(2,1)S(1)} fusion(bf16[2,512,8,128]{3,2,1,0:T(8,128)(2,1)} %bitcast.210, f32[2,8,128]{2,1,0:T(8,128)S(1)} %copy.268, f32[2,8,128]{2,1,0:T(8,128)S(1)} %copy_add_fusion, f32[2,8,128]{2,1,0:T(8,128)S(1)} %copy_maximum_fusion, f32[2,8,512,128]{3,2,1,0:T(8,128)} %copy-done.5, ...), kind=kOutput, calls=%fused_computation.13 | convolution fusion | flops 275775488 | bytes 8938496 | tf_op jit(solution)/shard_map/cqhd,ckhd->chqk/dot_general | solution.py:147
  162.2 4.6 %reshape.214 = bf16[8,128,1024]{2,1,0:T(8,128)(2,1)} reshape(bf16[2,512,8,128]{3,2,1,0:T(8,128)(2,1)} %copy.273) | data formatting | bytes 4194304 | tf_op jit(solution)/shard_map/reshape | solution.py:186
  166.7 2.9 convert_bitcast_fusion.2
  172.1 4.3 %all-to-all-start.2 = ((bf16[8,1,128,1024]{3,2,1,0:T(8,128)(2,1)}), bf16[8,1,128,1024]{3,2,1,0:T(8,128)(2,1)}, u32[]{:S(2)}, u32[]{:S(2)}) async-start(bf16[8,1,128,1024]{3,2,1,0:T(8,128)(2,1)} %copy.275), calls=%async_computation.2 | async-start | bytes 4194304 | tf_op jit(solution)/shard_map/all_to_all | solution.py:197
  176.5 5.2 %fusion.1 = bf16[2,8,128,1024]{2,3,0,1:T(8,128)(2,1)S(1)} fusion(f32[2,8,128]{2,0,1:T(2,128)S(1)} %copy.304, bf16[1024,8,128,1]{0,2,3,1:T(8,128)(2,1)S(1)} %bitcast.196, bf16[2,128,8,128]{1,3,0,2:T(8,128)(2,1)} %copy.286, f32[2,8,128]{2,0,1:T(2,128)S(1)} %copy.253, f32[2,8,128]{2,0,1:T(2,128)S(1)} %copy.251, f32[8,1024,2,128]{3,1,2,0:T(8,128)} %copy-done.2), kind=kOutput, calls=%fused_computation.3 | convolution fusion | flops 549453824 | bytes 15228928 | tf_op jit(solution)/shard_map/xswr,gwr->xwsg/dot_general | solution.py:141
  185.1 7.0 %fusion.5 = bf16[8,1024,128]{1,2,0:T(8,128)(2,1)} fusion(f32[8,1024,128,1]{1,2,3,0:T(8,128)S(1)} %fusion.110, bf16[2,128,8,128]{1,3,0,2:T(8,128)(2,1)S(1)} %copy-done.14, f32[8,1024,2,128]{3,1,2,0:T(8,128)} %copy-done.2, f32[2,8,128]{2,0,1:T(2,128)S(1)} %copy.253, f32[2,8,128]{2,0,1:T(2,128)S(1)} %copy.251), kind=kOutput, calls=%fused_computation.10 | convolution fusion | flops 548405248 | bytes 15220736 | tf_op jit(solution)/shard_map/irey,ierk->yrk/dot_general | solution.py:215
  192.2 3.9 %copy.287 = bf16[1024,1024]{1,0:T(8,128)(2,1)} copy(bf16[1024,1024]{0,1:T(8,128)(2,1)} %bitcast.211) | data formatting | bytes 4194304 | tf_op jit(solution)/shard_map/convert_element_type | solution.py:222
  201.1 4.2 %reshape.218 = bf16[8,128,1024]{2,1,0:T(8,128)(2,1)} reshape(bf16[2,512,8,128]{3,2,1,0:T(8,128)(2,1)} %copy.279) | data formatting | bytes 4194304 | tf_op jit(solution)/shard_map/reshape | solution.py:187
  205.3 2.9 convert_bitcast_fusion
  210.6 28.9 %all-to-all-done.2 = bf16[8,1,128,1024]{3,2,1,0:T(8,128)(2,1)} async-done(((bf16[8,1,128,1024]{3,2,1,0:T(8,128)(2,1)}), bf16[8,1,128,1024]{3,2,1,0:T(8,128)(2,1)}, u32[]{:S(2)}, u32[]{:S(2)}) %all-to-all-start.2) | async-done | bytes 2097184 | tf_op jit(solution)/shard_map/all_to_all | solution.py:197
  239.6 4.5 %all-to-all-start.3 = ((bf16[8,1,128,1024]{3,2,1,0:T(8,128)(2,1)}), bf16[8,1,128,1024]{3,2,1,0:T(8,128)(2,1)}, u32[]{:S(2)}, u32[]{:S(2)}) async-start(bf16[8,1,128,1024]{3,2,1,0:T(8,128)(2,1)} %copy.281), calls=%async_computation.3 | async-start | bytes 4194304 | tf_op jit(solution)/shard_map/all_to_all | solution.py:198
  245.4 3.2 %fusion.60 = f32[2,128,8,128]{1,3,0,2:T(8,128)S(1)} fusion(bf16[2,8,128,512]{2,3,1,0:T(8,128)(2,1)} %copy-done.9, bf16[2,512,8,128]{3,2,1,0:T(8,128)(2,1)} %bitcast.208), kind=kOutput, calls=%fused_computation.60 | convolution fusion | flops 268435456 | bytes 5242880 | tf_op jit(solution)/shard_map/chqk,ckhd->cqhd/dot_general | solution.py:164
  251.2 3.1 fusion.71
  257.1 36.1 %all-to-all-done.3 = bf16[8,1,128,1024]{3,2,1,0:T(8,128)(2,1)} async-done(((bf16[8,1,128,1024]{3,2,1,0:T(8,128)(2,1)}), bf16[8,1,128,1024]{3,2,1,0:T(8,128)(2,1)}, u32[]{:S(2)}, u32[]{:S(2)}) %all-to-all-start.3) | async-done | bytes 2097184 | tf_op jit(solution)/shard_map/all_to_all | solution.py:198
  293.1 3.1 fusion.74
  297.1 7.2 %all-reduce.2.cloned.1.call-done = bf16[128,1024]{1,0:T(8,128)(2,1)} async-done(((bf16[128,1024]{1,0:T(8,128)(2,1)}), bf16[128,1024]{1,0:T(8,128)(2,1)}) %all-reduce.2.cloned.1.call-update) | async-done | bytes 262160 | tf_op jit(solution)/shard_map/psum | solution.py:229
  (111 shorter events, 62.4 us)
Async XLA Ops:
  7.2 2.3 copy-start
  10.5 9.6 %copy-start.11 = (bf16[1,256,1024]{2,1,0:T(8,128)(2,1)S(1)}, bf16[1,256,1024]{2,1,0:T(8,128)(2,1)}, u32[]{:S(2)}) copy-start(bf16[1,256,1024]{2,1,0:T(8,128)(2,1)} %param.11) | copy-start | bytes 1572868
  13.0 72.3 %all-to-all-start = ((bf16[8,1,128,1024]{3,2,1,0:T(8,128)(2,1)}), bf16[8,1,128,1024]{3,2,1,0:T(8,128)(2,1)}, u32[]{:S(2)}, u32[]{:S(2)}) async-start(bf16[8,1,128,1024]{3,2,1,0:T(8,128)(2,1)} %copy.244), calls=%async_computation | async-start | bytes 4194304 | tf_op jit(solution)/shard_map/all_to_all | solution.py:76
  19.3 78.5 %all-gather.2.cloned.1.call-start = ((), (), s32[]{:S(2)}) async-start(), calls=%async_computation.5 | async-start | bytes 2359296 | tf_op jit(solution)/shard_map/all_gather | solution.py:55
  24.0 65.9 %copy-start.12 = (bf16[1,256,1024]{2,1,0:T(8,128)(2,1)S(1)}, bf16[1,256,1024]{2,1,0:T(8,128)(2,1)}, u32[]{:S(2)}) copy-start(bf16[1,256,1024]{2,1,0:T(8,128)(2,1)} %param.9) | copy-start | bytes 1572868
  26.5 63.9 %copy-start.13 = (bf16[1,256,1024]{2,1,0:T(8,128)(2,1)S(1)}, bf16[1,256,1024]{2,1,0:T(8,128)(2,1)}, u32[]{:S(2)}) copy-start(bf16[1,256,1024]{2,1,0:T(8,128)(2,1)} %param.12) | copy-start | bytes 1572868
  26.5 65.1 %copy-start.16 = (s32[16]{0:T(128)S(1)}, s32[16]{0:T(128)}, u32[]{:S(2)}) copy-start(s32[16]{0:T(128)} %param.16) | copy-start | bytes 196
  85.4 53.6 %all-to-all-start.1 = ((bf16[8,1,128,1024]{3,2,1,0:T(8,128)(2,1)}), bf16[8,1,128,1024]{3,2,1,0:T(8,128)(2,1)}, u32[]{:S(2)}, u32[]{:S(2)}) async-start(bf16[8,1,128,1024]{3,2,1,0:T(8,128)(2,1)} %copy.256), calls=%async_computation.1 | async-start | bytes 4194304 | tf_op jit(solution)/shard_map/all_to_all | solution.py:77
  90.0 1.7 copy-start.7
  103.3 4.6 %copy-start.5 = (f32[2,8,512,128]{3,2,1,0:T(8,128)}, f32[2,8,512,128]{3,2,1,0:T(8,128)S(1)}, u32[]{:S(2)}) copy-start(f32[2,8,512,128]{3,2,1,0:T(8,128)S(1)} %get-tuple-element.8) | copy-start | bytes 12582916
  104.6 3.2 %copy-start.2 = (f32[8,1024,2,128]{3,1,2,0:T(8,128)}, f32[8,1024,2,128]{3,1,2,0:T(8,128)S(1)}, u32[]{:S(2)}) copy-start(f32[8,1024,2,128]{3,1,2,0:T(8,128)S(1)} %get-tuple-element.10) | copy-start | bytes 25165828
  138.9 7.1 %slice-start = ((s8[8388608]{0:T(1024)(128)(4,1)}), s8[4194304]{0:T(1024)(128)(4,1)S(1)}, s32[]{:S(2)}) async-start(s8[8388608]{0:T(1024)(128)(4,1)} %bitcast.192), calls=%async_computation.8 | async-start | bytes 8388608
  142.0 3.2 %copy-start.6 = (bf16[2,8,128,512]{2,3,1,0:T(8,128)(2,1)S(1)}, bf16[2,8,128,512]{2,3,1,0:T(8,128)(2,1)}, u32[]{:S(2)}) copy-start(bf16[2,8,128,512]{2,3,1,0:T(8,128)(2,1)} %fusion.80) | copy-start | bytes 6291460
  143.2 2.9 slice-start.1
  153.5 4.6 %copy-start.8 = (bf16[32,8,8,128]{3,2,1,0:T(8,128)(2,1)S(1)}, bf16[32,8,8,128]{3,2,1,0:T(8,128)(2,1)}, u32[]{:S(2)}) copy-start(bf16[32,8,8,128]{3,2,1,0:T(8,128)(2,1)} %copy-done.7) | copy-start | bytes 1572868
  172.1 67.4 %all-to-all-start.2 = ((bf16[8,1,128,1024]{3,2,1,0:T(8,128)(2,1)}), bf16[8,1,128,1024]{3,2,1,0:T(8,128)(2,1)}, u32[]{:S(2)}, u32[]{:S(2)}) async-start(bf16[8,1,128,1024]{3,2,1,0:T(8,128)(2,1)} %copy.275), calls=%async_computation.2 | async-start | bytes 4194304 | tf_op jit(solution)/shard_map/all_to_all | solution.py:197
  176.5 78.7 %reduce-scatter.2.cloned.1.call-start = ((), (), s32[]{:S(2)}) async-start(), calls=%async_computation.6 | async-start | bytes 2359296 | tf_op jit(solution)/shard_map/reduce_scatter | solution.py:221
  181.7 2.0 copy-start.3
  183.6 1.5 copy-start.14
  208.2 35.9 %copy-start.15 = (bf16[2,128,8,128]{1,3,0,2:T(8,128)(2,1)S(1)}, bf16[2,128,8,128]{1,3,0,2:T(8,128)(2,1)}, u32[]{:S(2)}) copy-start(bf16[2,128,8,128]{1,3,0,2:T(8,128)(2,1)} %get-tuple-element.12) | copy-start | bytes 1572868
  239.6 53.6 %all-to-all-start.3 = ((bf16[8,1,128,1024]{3,2,1,0:T(8,128)(2,1)}), bf16[8,1,128,1024]{3,2,1,0:T(8,128)(2,1)}, u32[]{:S(2)}, u32[]{:S(2)}) async-start(bf16[8,1,128,1024]{3,2,1,0:T(8,128)(2,1)} %copy.281), calls=%async_computation.3 | async-start | bytes 4194304 | tf_op jit(solution)/shard_map/all_to_all | solution.py:198
  245.4 3.4 %copy-start.4 = (bf16[2,8,128,1024]{2,3,0,1:T(8,128)(2,1)S(1)}, bf16[2,8,128,1024]{2,3,0,1:T(8,128)(2,1)}, u32[]{:S(2)}) copy-start(bf16[2,8,128,1024]{2,3,0,1:T(8,128)(2,1)} %copy-done.3) | copy-start | bytes 12582916
  251.2 55.0 %copy-start.1 = (bf16[1,256,1024]{2,1,0:T(8,128)(2,1)S(1)}, bf16[1,256,1024]{2,1,0:T(8,128)(2,1)}, u32[]{:S(2)}) copy-start(bf16[1,256,1024]{2,1,0:T(8,128)(2,1)} %param.10) | copy-start | bytes 1572868
  256.1 48.2 %all-reduce.2.cloned.1.call-start = ((), (), s32[]{:S(2)}) async-start(), calls=%async_computation.7 | async-start | bytes 524288 | tf_op jit(solution)/shard_map/psum | solution.py:229
  (2 other events, 2.7 us)
Sparse Core Ops, SparseCore 0:
  23.1 56.3 all-gather.1
  196.3 49.0 reduce-scatter.1
  259.9 44.3 all-reduce.1
where the time goes:
time: 318 us; the launch traced here: 313 us
  waiting for transfers between devices  160 us (50%)
  matrix products  53.4 us (17%)
  local copies, waits for them, and re-layouts  52.3 us (16%)
  starting transfers between devices  19.8 us (6%)
  between operations  14.4 us (5%)
  other arithmetic  12.4 us (4%)
    all_to_all x1, waiting for transfers between devices, shards(): lax.all_to_all(send_keys, 'seq', split_axis=0, concat_axis=0, tiled=True)  58.8 us
    all_to_all x1, waiting for transfers between devices, shards(): lax.all_to_all(back_values, 'seq', split_axis=0, concat_axis=0, tiled=True)  36.1 us
    all_to_all x1, waiting for transfers between devices, shards(): lax.all_to_all(back_keys, 'seq', split_axis=0, concat_axis=0, tiled=True)  28.9 us
    all_to_all x1, waiting for transfers between devices, shards(): lax.all_to_all(send_values, 'seq', split_axis=0, concat_axis=0, tiled=True)  28.8 us
    unnamed x45, local copies, waits for them, and re-layouts  12 us
    psum x1, waiting for transfers between devices, shards(): lax.psum(row_grads.astype(jnp.bfloat16), 'batch').astype(jnp.float32)  7.19 us
    dot_general x1, matrix products, shards(): jnp.einsum('irey,ierk->yrk', memory_attention_weight, head_output_gradien...  7.02 us
  transfers between devices with their start and end apart: 7, of which 5 were waited for; matrix products, arithmetic and copies ran while one was open for 24% of the time, Pallas kernels for 0%

commit v1 on v0

v1 whole, which is shorter than its diff:
```python
import functools
import math

import jax
import jax.numpy as jnp
from jax import lax
from jax.experimental import pallas as pl
from jax.experimental.pallas import tpu as pltpu
from jax.sharding import PartitionSpec as P

HEADS = 8
HD = 128
BLK = 128
MEM = 1024
GROUPS = 2
F32 = jnp.float32
BF16 = jnp.bfloat16


def dot_nt(a, b):
    return lax.dot_general(a, b, (((1,), (1,)), ((), ())), preferred_element_type=F32)


def dot_tn(a, b):
    return lax.dot_general(a, b, (((0,), (0,)), ((), ())), preferred_element_type=F32)


def dot_nn(a, b):
    return lax.dot_general(a, b, (((1,), (0,)), ((), ())), preferred_element_type=F32)


def head_kernel(
    near_width,
    dev_ref,
    slot_ref,
    count_ref,
    q_ref,
    g_ref,
    kv_ref,
    mem_ref,
    second_ref,
    att_ref,
    qg_ref,
    out_ref,
    spread_ref,
):
    tokens = q_ref.shape[0]
    blocks = tokens // BLK
    n = kv_ref.shape[0]
    rows_dev = MEM // n
    scale = 1.0 / math.sqrt(HD)
    block_scale = 1.0 / math.sqrt(BLK)
    to_exp2 = scale * math.log2(math.e)
    values = kv_ref[:, tokens:, :].astype(F32).reshape(n, blocks, BLK, HD)
    sums = jnp.sum(values, axis=2)
    second = second_ref[...].reshape(n, rows_dev, 1) > 0.5
    add = jnp.where(second, sums[:, 1:2, :], sums[:, 0:1, :])
    mem_keys = (mem_ref[...].reshape(n, rows_dev, HD) + add * block_scale).astype(BF16)
    mem_keys = mem_keys.reshape(MEM, HD)
    term = jnp.zeros((MEM, HD), F32)
    parts = []
    for l in range(blocks):
        rows = slice(l * BLK, (l + 1) * BLK)
        q = q_ref[rows, :]
        g = g_ref[rows, :]
        keys, vals = [], []
        for j in range(near_width):
            d, s = dev_ref[l, j], slot_ref[l, j]
            keys.append(kv_ref[d, pl.ds(pl.multiple_of(s * BLK, BLK), BLK), :])
            vals.append(kv_ref[d, pl.ds(pl.multiple_of(tokens + s * BLK, BLK), BLK), :])
        near_keys = jnp.concatenate(keys, axis=0)
        near_vals = jnp.concatenate(vals, axis=0)
        s_mem = dot_nt(q, mem_keys)
        s_near = dot_nt(q, near_keys)
        live = lax.broadcasted_iota(jnp.int32, s_near.shape, 1) < count_ref[l] * BLK
        s_near = jnp.where(live, s_near, -jnp.inf)
        top = jnp.maximum(
            jnp.max(s_mem, axis=1, keepdims=True), jnp.max(s_near, axis=1, keepdims=True)
        )
        e_mem = jnp.exp2((s_mem - top) * to_exp2)
        e_near = jnp.exp2((s_near - top) * to_exp2)
        total = jnp.sum(e_mem, axis=1, keepdims=True) + jnp.sum(e_near, axis=1, keepdims=True)
        inv = 1.0 / total
        p_mem = e_mem * inv
        p_near = e_near * inv
        w_mem = p_mem.astype(BF16)
        w_near = p_near.astype(BF16)
        att = (dot_nn(w_mem, mem_keys) + dot_nn(w_near, near_vals)).astype(BF16)
        att_ref[rows, :] = att
        gdot = jnp.sum(g.astype(F32) * att.astype(F32), axis=1, keepdims=True)
        ds_mem = (p_mem * (dot_nt(g, mem_keys) - gdot)).astype(BF16)
        ds_near = (p_near * (dot_nt(g, near_vals) - gdot)).astype(BF16)
        qg_ref[rows, :] = (
            (dot_nn(ds_mem, mem_keys) + dot_nn(ds_near, near_keys)) * scale
        ).astype(BF16)
        term = term + dot_tn(ds_mem, q) * scale + dot_tn(w_mem, g)
        parts.append((dot_tn(ds_near, q) * scale, dot_tn(w_near, g)))
    rows3 = term.reshape(n, rows_dev, HD)
    first_sum = jnp.sum(jnp.where(second, 0.0, rows3), axis=1, keepdims=True) * block_scale
    second_sum = jnp.sum(jnp.where(second, rows3, 0.0), axis=1, keepdims=True) * block_scale
    spread = jnp.concatenate([first_sum, second_sum], axis=1)
    spread_ref[...] = spread
    out_ref[:, 0:tokens, :] = jnp.zeros((n, tokens, HD), BF16)
    for s in range(blocks):
        out_ref[:, tokens + s * BLK : tokens + (s + 1) * BLK, :] = jnp.broadcast_to(
            spread[:, s : s + 1, :], (n, BLK, HD)
        ).astype(BF16)
    out_ref[:, 2 * tokens :, :] = rows3.astype(BF16)
    for l in range(blocks):
        for j in range(near_width):
            d, s = dev_ref[l, j], slot_ref[l, j]
            here = slice(j * BLK, (j + 1) * BLK)
            row = spread_ref[d, pl.ds(s, 1), :]
            out_ref[d, pl.ds(pl.multiple_of(s * BLK, BLK), BLK), :] = parts[l][0][here].astype(BF16)
            out_ref[d, pl.ds(pl.multiple_of(tokens + s * BLK, BLK), BLK), :] = (
                parts[l][1][here] + row
            ).astype(BF16)


def attend_group(group, heads, tables, queries, out_grad, kv, memory, second):
    tokens = queries.shape[0]
    n = kv.shape[0]
    near_width = tables[0].shape[1]
    rows_dev = MEM // n
    first = group * heads
    width = heads * HD
    whole = lambda h, *_: (0, first + h)
    part = lambda h, *_: (0, h)
    part3 = lambda h, *_: (0, 0, h)
    keys = MEM + near_width * BLK
    return pl.pallas_call(
        functools.partial(head_kernel, near_width),
        out_shape=(
            jax.ShapeDtypeStruct((tokens, width), BF16),
            jax.ShapeDtypeStruct((tokens, width), BF16),
            jax.ShapeDtypeStruct((n, 2 * tokens + rows_dev, width), BF16),
        ),
        grid_spec=pltpu.PrefetchScalarGridSpec(
            num_scalar_prefetch=3,
            grid=(heads,),
            in_specs=[
                pl.BlockSpec((tokens, HD), whole),
                pl.BlockSpec((tokens, HD), whole),
                pl.BlockSpec((n, 2 * tokens, HD), part3),
                pl.BlockSpec((MEM, HD), whole),
                pl.BlockSpec((MEM, 1), lambda h, *_: (0, 0)),
            ],
            out_specs=(
                pl.BlockSpec((tokens, HD), part),
                pl.BlockSpec((tokens, HD), part),
                pl.BlockSpec((n, 2 * tokens + rows_dev, HD), part3),
            ),
            scratch_shapes=[pltpu.VMEM((n, tokens // BLK, HD), F32)],
        ),
        compiler_params=pltpu.CompilerParams(
            dimension_semantics=("arbitrary",), vmem_limit_bytes=50 * 1024 * 1024
        ),
        cost_estimate=pl.CostEstimate(
            flops=12 * tokens * keys * width,
            bytes_accessed=n * tokens * width * 10,
            transcendentals=heads * tokens * keys,
        ),
    )(*tables, queries, out_grad, kv, memory, second)


def shards(
    queries,
    key_states,
    value_states,
    out_grad,
    memory,
    near_device,
    near_slot,
    near_count,
    writer_block,
):
    my_index = lax.axis_index("seq")
    tokens = queries.shape[1]
    local_blocks = tokens // BLK
    heads = HEADS // GROUPS
    width = heads * HD
    mine = lambda t: lax.dynamic_slice_in_dim(t, my_index * local_blocks, local_blocks, 0)
    tables = (mine(near_device), mine(near_slot), mine(near_count))
    second = (writer_block % local_blocks).astype(F32).reshape(MEM, 1)
    gathered = []
    for group in range(GROUPS):
        cols = slice(group * width, (group + 1) * width)
        packed = jnp.concatenate([key_states[0][:, cols], value_states[0][:, cols]], axis=0)
        gathered.append(lax.all_gather(packed, "seq", axis=0, tiled=False))
    results = []
    for group in range(GROUPS):
        att, qg, out = attend_group(
            group, heads, tables, queries[0], out_grad[0], gathered[group], memory, second
        )
        got = lax.psum_scatter(out, "seq", scatter_dimension=0, tiled=False)
        results.append((att, qg, got[:tokens], got[tokens : 2 * tokens], got[2 * tokens :]))
    att, qg, kg, vg, rows = [jnp.concatenate(c, axis=1) for c in zip(*results)]
    memory_grad = lax.psum(rows, "batch").astype(F32)
    return (att[None], qg[None], kg[None], vg[None], memory_grad)


def solution(mesh):
    placed = (P("batch", "seq", None),) * 4 + (P(),) * 5
    return jax.shard_map(
        shards,
        mesh=mesh,
        in_specs=placed,
        out_specs=(P("batch", "seq", None),) * 4 + (P("seq", None),),
        check_vma=False,
    )
```

time: 318 us -> 283 us (0.89); the launches traced: 313 us -> 283 us
  waiting for transfers between devices: 160 us -> 227 us
  matrix products: 53.4 us -> 0 us
  local copies, waits for them, and re-layouts: 52.3 us -> 5.9 us
  Pallas kernels: 0 us -> 27.6 us
  starting transfers between devices: 19.8 us -> 0.21 us
  other arithmetic: 12.4 us -> 7.63 us
    all_to_all x4 -> x0, waiting for transfers between devices: 153 us -> none  [the longest x1 58.8 us: shards(): lax.all_to_all(send_keys, 'seq', split_axis=0, concat_axis=0, tiled=True)]
    reduce_scatter x1 -> x2, waiting for transfers between devices: 0.01 us -> 105 us  [shards(): got = lax.psum_scatter(out, 'seq', scatter_dimension=0, tiled=False)]
    all_gather x1 -> x2, waiting for transfers between devices: 0.01 us -> 83.3 us  [shards(): gathered.append(lax.all_gather(packed, 'seq', axis=0, tiled=False))]
    dot_general x21 -> x0, matrix products: 53.4 us -> none  [the longest x1 7.02 us: shards(): jnp.einsum('irey,ierk->yrk', memory_attention_weight, head_output_gradien...]
    psum x1, waiting for transfers between devices: 7.19 us -> 39.1 us  [shards(): memory_grad = lax.psum(rows, 'batch').astype(F32)]
    pallas_call x0 -> x2, Pallas kernels: none -> 27.6 us  [attend_group(): pl.pallas_call(functools.partial(head_kernel, near_width), out_shape=(jax...]
    all_to_all x4 -> x0, starting transfers between devices: 19.7 us -> none  [the longest x1 6.32 us: shards(): lax.all_to_all(send_keys, 'seq', split_axis=0, concat_axis=0, tiled=True)]
    convert_element_type x11 -> x0, local copies, waits for them, and re-layouts: 19 us -> none  [the longest x1 3.95 us: shards(): term.reshape(lax.axis_size('seq') * rows_dev, row_width)]
  transfers between devices with their start and end apart: 7 -> 5, of which waited for: 5 -> 5; matrix products, arithmetic and copies ran while one was open for 24% -> 3% of each run, Pallas kernels for 0% -> 10%
where the time goes in v1:
time: 283 us
  waiting for transfers between devices  227 us (80%)
  Pallas kernels  27.6 us (10%)
  between operations  13.9 us (5%)
  other arithmetic  7.63 us (3%)
  local copies, waits for them, and re-layouts  5.9 us (2%)
    reduce_scatter x2, waiting for transfers between devices, shards(): got = lax.psum_scatter(out, 'seq', scatter_dimension=0, tiled=False)  105 us
    all_gather x2, waiting for transfers between devices, shards(): gathered.append(lax.all_gather(packed, 'seq', axis=0, tiled=False))  83.3 us
    psum x1, waiting for transfers between devices, shards(): memory_grad = lax.psum(rows, 'batch').astype(F32)  39.1 us
    pallas_call x2, Pallas kernels, attend_group(): pl.pallas_call(functools.partial(head_kernel, near_width), out_shape=(jax...  27.6 us
  transfers between devices with their start and end apart: 5, of which 5 were waited for; matrix products, arithmetic and copies ran while one was open for 3% of the time, Pallas kernels for 10%

profile of v1, /device:TPU:0, one launch (start us, length us, event | category | flops | bytes accessed | tf_op | source)
XLA Modules:
  0.0 282.6 jit_solution(4066686300578822036)
XLA Ops:
  7.3 1.4 fusion.2
  8.6 0.8 pad_maximum_fusion
  9.5 0.8 pad_maximum_fusion.1
  10.5 0.1 constant_dynamic-slice_fusion
  10.5 0.1 copy.20.dev_ref
  10.6 0.1 copy.21.slot_ref
  10.8 0.2 copy.18.second_ref
  11.1 49.1 %all-gather.5.cloned.1.call-done = bf16[4096,512]{1,0:T(8,128)(2,1)} async-done(((bf16[512,512]{1,0:T(8,128)(2,1)}), bf16[4096,512]{1,0:T(8,128)(2,1)}) %all-gather.5.cloned.1.call-update) | async-done | bytes 4194320 | tf_op jit(solution)/shard_map/all_gather | solution.py:189
  60.1 13.8 %shard_map.128 = (bf16[256,512]{1,0:T(8,128)(2,1)S(1)}, bf16[256,512]{1,0:T(8,128)(2,1)S(1)}, bf16[8,640,512]{2,1,0:T(8,128)(2,1)}) custom-call(s32[2,4]{1,0:T(2,128)S(1)} %copy.20.dev_ref, s32[2,4]{1,0:T(2,128)S(1)} %copy.21.slot_ref, s32[2]{0:T(128)S(1)} %dynamic_slice.11.count_ref, bf16[256,1024]{1,0:T(8,128)(2,1)S(1)} %bitcast.27, ...), custom_call_target="tpu_custom_call" | custom-call | flops 2415919104 | bytes 10485760 | tf_op jit(solution)/shard_map/pallas_call | solution.py:131
  74.0 34.2 %all-gather.7.cloned.1.call-done = bf16[4096,512]{1,0:T(8,128)(2,1)} async-done(((bf16[512,512]{1,0:T(8,128)(2,1)}), bf16[4096,512]{1,0:T(8,128)(2,1)}) %all-gather.7.cloned.1.call-update) | async-done | bytes 4194320 | tf_op jit(solution)/shard_map/all_gather | solution.py:189
  108.2 13.8 %shard_map.129 = (bf16[256,512]{1,0:T(8,128)(2,1)S(1)}, bf16[256,512]{1,0:T(8,128)(2,1)S(1)}, bf16[8,640,512]{2,1,0:T(8,128)(2,1)}) custom-call(s32[2,4]{1,0:T(2,128)S(1)} %copy.20.dev_ref, s32[2,4]{1,0:T(2,128)S(1)} %copy.21.slot_ref, s32[2]{0:T(128)S(1)} %dynamic_slice.11.count_ref, bf16[256,1024]{1,0:T(8,128)(2,1)S(1)} %bitcast.28, ...), custom_call_target="tpu_custom_call" | custom-call | flops 2415919104 | bytes 10485760 | tf_op jit(solution)/shard_map/pallas_call | solution.py:131
  122.1 0.9 maximum_bitcast_fusion.1
  123.0 0.9 maximum_bitcast_fusion
  123.8 45.3 %reduce-scatter.3.cloned.1.call-done = bf16[1,640,512]{2,1,0:T(8,128)(2,1)} async-done(((bf16[8,640,512]{2,1,0:T(8,128)(2,1)}), bf16[1,640,512]{2,1,0:T(8,128)(2,1)}) %reduce-scatter.3.cloned.1.call-update) | async-done | bytes 655376 | tf_op jit(solution)/shard_map/reduce_scatter | solution.py:195
  169.2 0.9 slice_bitcast_fusion.5
  170.1 59.5 %reduce-scatter.5.cloned.1.call-done = bf16[1,640,512]{2,1,0:T(8,128)(2,1)} async-done(((bf16[8,640,512]{2,1,0:T(8,128)(2,1)}), bf16[1,640,512]{2,1,0:T(8,128)(2,1)}) %reduce-scatter.5.cloned.1.call-update) | async-done | bytes 655376 | tf_op jit(solution)/shard_map/reduce_scatter | solution.py:195
  229.6 0.9 slice_bitcast_fusion.4
  230.5 0.7 pad_maximum_fusion.2
  231.3 1.1 slice_bitcast_fusion.1
  232.4 1.1 slice_bitcast_fusion
  233.4 0.9 maximum_bitcast_fusion.3
  234.3 0.9 maximum_bitcast_fusion.2
  235.2 39.1 %all-reduce.2.cloned.1.call-done = bf16[128,1024]{1,0:T(8,128)(2,1)} async-done(((bf16[128,1024]{1,0:T(8,128)(2,1)}), bf16[128,1024]{1,0:T(8,128)(2,1)}) %all-reduce.2.cloned.1.call-update) | async-done | bytes 262160 | tf_op jit(solution)/shard_map/psum | solution.py:198
  274.3 1.8 convert_element_type.7
  (24 shorter events, 0.4 us)
Async XLA Ops:
  7.2 3.3 %copy-start.4 = (s32[16,4]{0,1:T(4,128)S(1)}, s32[16,4]{0,1:T(4,128)}, u32[]{:S(2)}) copy-start(s32[16,4]{0,1:T(4,128)} %param.14) | copy-start | bytes 772
  7.2 3.3 %copy-start.3 = (s32[16,4]{0,1:T(4,128)S(1)}, s32[16,4]{0,1:T(4,128)}, u32[]{:S(2)}) copy-start(s32[16,4]{0,1:T(4,128)} %param.15) | copy-start | bytes 772
  7.2 3.5 %copy-start.5 = (s32[16]{0:T(128)S(1)}, s32[16]{0:T(128)}, u32[]{:S(2)}) copy-start(s32[16]{0:T(128)} %param.16) | copy-start | bytes 196
  7.2 3.6 %copy-start.2 = (s32[1024]{0:T(1024)S(1)}, s32[1024]{0:T(1024)}, u32[]{:S(2)}) copy-start(s32[1024]{0:T(1024)} %param.17) | copy-start | bytes 12292
  7.2 52.9 %copy-start = (bf16[1,256,1024]{2,1,0:T(8,128)(2,1)S(1)}, bf16[1,256,1024]{2,1,0:T(8,128)(2,1)}, u32[]{:S(2)}) copy-start(bf16[1,256,1024]{2,1,0:T(8,128)(2,1)} %param.9) | copy-start | bytes 1572868
  7.2 52.9 %copy-start.1 = (bf16[1,256,1024]{2,1,0:T(8,128)(2,1)S(1)}, bf16[1,256,1024]{2,1,0:T(8,128)(2,1)}, u32[]{:S(2)}) copy-start(bf16[1,256,1024]{2,1,0:T(8,128)(2,1)} %param.12) | copy-start | bytes 1572868
  7.2 52.9 %all-gather.5.cloned.1.call-start = ((), (), s32[]{:S(2)}) async-start(), calls=%async_computation.5 | async-start | bytes 4718592 | tf_op jit(solution)/shard_map/all_gather | solution.py:189
  9.5 98.7 %all-gather.7.cloned.1.call-start = ((), (), s32[]{:S(2)}) async-start(), calls=%async_computation.6 | async-start | bytes 4718592 | tf_op jit(solution)/shard_map/all_gather | solution.py:189
  10.4 158.8 %reduce-scatter.3.cloned.1.call-start = ((), (), s32[]{:S(2)}) async-start(), calls=%async_computation.2 | async-start | bytes 5898240 | tf_op jit(solution)/shard_map/reduce_scatter | solution.py:195
  73.9 155.7 %reduce-scatter.5.cloned.1.call-start = ((), (), s32[]{:S(2)}) async-start(), calls=%async_computation.3 | async-start | bytes 5898240 | tf_op jit(solution)/shard_map/reduce_scatter | solution.py:195
  122.1 152.3 %all-reduce.2.cloned.1.call-start = ((), (), s32[]{:S(2)}) async-start(), calls=%async_computation.4 | async-start | bytes 524288 | tf_op jit(solution)/shard_map/psum | solution.py:198
Sparse Core Ops, SparseCore 0:
  10.2 49.8 all-gather.4
  62.3 45.8 all-gather.6
  110.5 58.5 reduce-scatter.2
  171.3 58.2 reduce-scatter.4
  233.0 41.2 all-reduce.1

commit v2 on v1

--- a/solution.py
+++ b/solution.py
@@ -199,10 +199,445 @@
     return (att[None], qg[None], kg[None], vg[None], memory_grad)
 
 
+MESH = pl.DeviceIdType.MESH
+
+
+def fused_kernel(
+    lines,
+    peers,
+    q_ref,
+    k_ref,
+    v_ref,
+    g_ref,
+    mem_ref,
+    second_ref,
+    bias_ref,
+    slot_ref,
+    att_ref,
+    qg_ref,
+    kg_ref,
+    vg_ref,
+    mg_ref,
+    kv,
+    own,
+    sib,
+    ups,
+    downs,
+    rows_own,
+    rows_got,
+    up_send,
+    down_send,
+    share_send,
+    kv_recv,
+    sib_send,
+    sib_recv,
+    ups_send,
+    ups_recv,
+    downs_send,
+    downs_recv,
+    rows_send,
+    rows_recv,
+):
+    n = 2 * lines
+    tokens = q_ref.shape[0]
+    rows_dev = MEM // n
+    scale = 1.0 / math.sqrt(HD)
+    block_scale = 1.0 / math.sqrt(BLK)
+    to_exp2 = scale * math.log2(math.e)
+    me = lax.axis_index("seq")
+    b = lax.axis_index("batch")
+    z, core = me // 2, me % 2
+    last = lines - 1
+
+    def at(zz, cc):
+        return (b, zz * 2 + cc)
+
+    barrier = pltpu.get_barrier_semaphore()
+
+    @pl.when(z < last)
+    def _():
+        pl.semaphore_signal(barrier, inc=1, device_id=at(z + 1, core), device_id_type=MESH)
+
+    @pl.when(z > 0)
+    def _():
+        pl.semaphore_signal(barrier, inc=1, device_id=at(z - 1, core), device_id_type=MESH)
+
+    pl.semaphore_signal(barrier, inc=1, device_id=at(z, 1 - core), device_id_type=MESH)
+    for p in range(1, peers):
+        pl.semaphore_signal(barrier, inc=1, device_id=((b + p) % peers, me), device_id_type=MESH)
+    edges = jnp.where(z < last, 1, 0) + jnp.where(z > 0, 1, 0)
+    pl.semaphore_wait(barrier, edges + peers)
+
+    def send(src, dst, s, r, dev):
+        return pltpu.make_async_remote_copy(
+            src_ref=src, dst_ref=dst, send_sem=s, recv_sem=r, device_id=dev, device_id_type=MESH
+        )
+
+    def kv_up(h, o):
+        i = o * 2 + core
+        return send(
+            kv.at[h, i], kv.at[h, i], up_send.at[h, o], kv_recv.at[h, i], at((z + 1) % lines, core)
+        )
+
+    def kv_down(h, o):
+        i = o * 2 + core
+        return send(
+            kv.at[h, i],
+            kv.at[h, i],
+            down_send.at[h, o],
+            kv_recv.at[h, i],
+            at((z + last) % lines, core),
+        )
+
+    def kv_share(h, o):
+        i = o * 2 + core
+        return send(
+            kv.at[h, i], kv.at[h, i], share_send.at[h, o], kv_recv.at[h, i], at(z, 1 - core)
+        )
+
+    def kv_got(h, o, c):
+        i = o * 2 + c
+        send(
+            kv.at[h, i], kv.at[h, i], share_send.at[h, o], kv_recv.at[h, i], at(z, 1 - core)
+        ).wait_recv()
+
+    def sib_copy(h):
+        return send(own.at[h, 1 - core], sib.at[h], sib_send.at[h], sib_recv.at[h], at(z, 1 - core))
+
+    def sum_up(h, d):
+        return send(
+            own.at[h, core, d],
+            ups.at[h, d],
+            ups_send.at[h, d],
+            ups_recv.at[h, d],
+            at((z + 1) % lines, core),
+        )
+
+    def sum_down(h, d):
+        return send(
+            own.at[h, core, d],
+            downs.at[h, d],
+            downs_send.at[h, d],
+            downs_recv.at[h, d],
+            at((z + last) % lines, core),
+        )
+
+    def row_copy(h, p):
+        return send(
+            rows_own.at[h],
+            rows_got.at[h, p],
+            rows_send.at[h, p],
+            rows_recv.at[h, p],
+            ((b + p + 1) % peers, me),
+        )
+
+    def lanes(h):
+        return pl.ds(pl.multiple_of(h * HD, HD), HD)
+
+    def gather_first(h):
+        kv[h, me, 0:tokens, :] = k_ref[:, lanes(h)]
+        kv[h, me, tokens : 2 * tokens, :] = v_ref[:, lanes(h)]
+
+        @pl.when(z < last)
+        def _():
+            kv_up(h, z).start()
+
+        @pl.when(z > 0)
+        def _():
+            kv_down(h, z).start()
+
+        kv_share(h, z).start()
+
+    def gather_next(h, k):
+        @pl.when(z >= k)
+        def _():
+            kv_got(h, z - k, core)
+
+            @pl.when(z < last)
+            def _():
+                kv_up(h, z - k).start()
+
+            kv_share(h, z - k).start()
+
+        @pl.when(z + k <= last)
+        def _():
+            kv_got(h, z + k, core)
+
+            @pl.when(z > 0)
+            def _():
+                kv_down(h, z + k).start()
+
+            kv_share(h, z + k).start()
+
+    def compute(h):
+        for o in range(lines):
+            kv_got(h, o, 1 - core)
+        q = q_ref[:, lanes(h)]
+        g = g_ref[:, lanes(h)]
+        values = kv[h, :, tokens:, :].astype(F32).reshape(n, 2, BLK, HD)
+        sums = jnp.sum(values, axis=2)
+        second = second_ref[...].reshape(n, rows_dev, 1) > 0.5
+        add = jnp.where(second, sums[:, 1:2, :], sums[:, 0:1, :])
+        mem_keys = (mem_ref[:, lanes(h)].reshape(n, rows_dev, HD) + add * block_scale).astype(BF16)
+        mem_keys = mem_keys.reshape(MEM, HD)
+        keys, vals = [], []
+        for d in range(n):
+            pick = slot_ref[d : d + 1, :] > 0.5
+            pair = lambda start: jnp.where(
+                pick,
+                kv[h, d, start + BLK : start + 2 * BLK, :].astype(F32),
+                kv[h, d, start : start + BLK, :].astype(F32),
+            ).astype(BF16)
+            keys.append(pair(0))
+            vals.append(pair(tokens))
+        near_keys = jnp.concatenate(keys, axis=0)
+        near_vals = jnp.concatenate(vals, axis=0)
+        bias = jnp.concatenate(
+            [jnp.broadcast_to(bias_ref[l : l + 1, :], (BLK, n * BLK)) for l in range(2)], axis=0
+        )
+        s_mem = dot_nt(q, mem_keys)
+        s_near = dot_nt(q, near_keys) + bias
+        top = jnp.maximum(
+            jnp.max(s_mem, axis=1, keepdims=True), jnp.max(s_near, axis=1, keepdims=True)
+        )
+        e_mem = jnp.exp2((s_mem - top) * to_exp2)
+        e_near = jnp.exp2((s_near - top) * to_exp2)
+        inv = 1.0 / (
+            jnp.sum(e_mem, axis=1, keepdims=True) + jnp.sum(e_near, axis=1, keepdims=True)
+        )
+        p_mem = e_mem * inv
+        p_near = e_near * inv
+        w_mem = p_mem.astype(BF16)
+        w_near = p_near.astype(BF16)
+        att = (dot_nn(w_mem, mem_keys) + dot_nn(w_near, near_vals)).astype(BF16)
+        att_ref[:, lanes(h)] = att
+        gdot = jnp.sum(g.astype(F32) * att.astype(F32), axis=1, keepdims=True)
+        ds_mem = (p_mem * (dot_nt(g, mem_keys) - gdot)).astype(BF16)
+        ds_near = (p_near * (dot_nt(g, near_vals) - gdot)).astype(BF16)
+        qg_ref[:, lanes(h)] = (
+            (dot_nn(ds_mem, mem_keys) + dot_nn(ds_near, near_keys)) * scale
+        ).astype(BF16)
+        rows3 = (dot_tn(ds_mem, q) * scale + dot_tn(w_mem, g)).reshape(n, rows_dev, HD)
+        first_sum = jnp.sum(jnp.where(second, 0.0, rows3), axis=1, keepdims=True) * block_scale
+        second_sum = jnp.sum(jnp.where(second, rows3, 0.0), axis=1, keepdims=True) * block_scale
+        key_part = dot_tn(ds_near, q) * scale
+        value_part = dot_tn(w_near, g)
+        for d in range(n):
+            here = slice(d * BLK, (d + 1) * BLK)
+            pick = slot_ref[d : d + 1, :] > 0.5
+            dk, dv = key_part[here], value_part[here]
+            dz, dc = d // 2, d % 2
+            own[h, dc, dz, 0:BLK, :] = jnp.where(pick, 0.0, dk).astype(BF16)
+            own[h, dc, dz, BLK : 2 * BLK, :] = jnp.where(pick, dk, 0.0).astype(BF16)
+            own[h, dc, dz, tokens : tokens + BLK, :] = (
+                jnp.where(pick, 0.0, dv) + first_sum[d]
+            ).astype(BF16)
+            own[h, dc, dz, tokens + BLK : 2 * tokens, :] = (
+                jnp.where(pick, dv, 0.0) + second_sum[d]
+            ).astype(BF16)
+            own[h, dc, dz, 2 * tokens :, :] = rows3[d].astype(BF16)
+        sib_copy(h).start()
+
+    def plus(a, c):
+        return a.astype(F32) + c.astype(F32)
+
+    def send_up(h, zz):
+        @pl.when(z == zz)
+        def _():
+            for d in range(zz + 1, lines):
+                sum_up(h, d).start()
+
+    def send_down(h, zz):
+        @pl.when(z == zz)
+        def _():
+            for d in range(zz):
+                sum_down(h, d).start()
+
+    def sum_first(h):
+        sib_copy(h).wait_recv()
+        own[h, core] = plus(own[h, core], sib[h]).astype(BF16)
+        send_up(h, 0)
+        send_down(h, last)
+
+    def sum_next(h, k):
+        @pl.when(z == k)
+        def _():
+            for d in range(k + 1, lines):
+                sum_up(h, d).wait_recv()
+                own[h, core, d] = plus(own[h, core, d], ups[h, d]).astype(BF16)
+                sum_up(h, d).start()
+
+        @pl.when(z == last - k)
+        def _():
+            for d in range(last - k):
+                sum_down(h, d).wait_recv()
+                own[h, core, d] = plus(own[h, core, d], downs[h, d]).astype(BF16)
+                sum_down(h, d).start()
+
+    def write_sums(h, total):
+        kg_ref[:, lanes(h)] = total[0:tokens].astype(BF16)
+        vg_ref[:, lanes(h)] = total[tokens : 2 * tokens].astype(BF16)
+        rows_own[h] = total[2 * tokens :].astype(BF16)
+
+    def finish(h):
+        @pl.when(z > 0)
+        def _():
+            sum_up(h, z).wait_recv()
+
+        @pl.when(z < last)
+        def _():
+            sum_down(h, z).wait_recv()
+
+        @pl.when(z == 0)
+        def _():
+            write_sums(h, plus(own[h, core, 0], downs[h, 0]))
+
+        @pl.when(z == last)
+        def _():
+            write_sums(h, plus(own[h, core, last], ups[h, last]))
+
+        @pl.when(jnp.logical_and(z > 0, z < last))
+        def _():
+            write_sums(h, plus(own[h, core, z], ups[h, z]) + downs[h, z].astype(F32))
+
+        for p in range(peers - 1):
+            row_copy(h, p).start()
+
+    def write_rows(h):
+        total = rows_own[h].astype(F32)
+        for p in range(peers - 1):
+            row_copy(h, p).wait_recv()
+            total = total + rows_got[h, p].astype(F32)
+        mg_ref[:, lanes(h)] = total
+
+    stages = [(0, gather_first)]
+    for k in range(1, lines):
+        stages.append((k, functools.partial(gather_next, k=k)))
+    stages.append((lines + 1, sum_first))
+    for k in range(1, last):
+        stages.append((lines + 1 + k, functools.partial(sum_next, k=k)))
+    stages.append((2 * lines, finish))
+    stages.append((2 * lines + 1, write_rows))
+    stages.append((lines, compute))
+
+    def tick(t, carry):
+        for lag, stage in stages:
+
+            @pl.when(jnp.logical_and(t >= lag, t < HEADS + lag))
+            def _(lag=lag, stage=stage):
+                stage(t - lag)
+
+        return carry
+
+    lax.fori_loop(0, HEADS + 2 * lines + 2, tick, 0)
+
+    def drain(h, carry):
+        for o in range(lines):
+            kv_share(h, o).wait_send()
+
+            @pl.when(jnp.logical_and(z < last, o <= z))
+            def _(o=o):
+                kv_up(h, o).wait_send()
+
+            @pl.when(jnp.logical_and(z > 0, o >= z))
+            def _(o=o):
+                kv_down(h, o).wait_send()
+
+            @pl.when(o > z)
+            def _(o=o):
+                sum_up(h, o).wait_send()
+
+            @pl.when(o < z)
+            def _(o=o):
+                sum_down(h, o).wait_send()
+
+        sib_copy(h).wait_send()
+        for p in range(peers - 1):
+            row_copy(h, p).wait_send()
+        return carry
+
+    lax.fori_loop(0, HEADS, drain, 0)
+
+
+def fused(
+    queries,
+    key_states,
+    value_states,
+    out_grad,
+    memory,
+    near_device,
+    near_slot,
+    near_count,
+    writer_block,
+):
+    me = lax.axis_index("seq")
+    n = lax.axis_size("seq")
+    peers = lax.axis_size("batch")
+    lines = n // 2
+    tokens = queries.shape[1]
+    width = queries.shape[2]
+    near_width = near_device.shape[1]
+    rows_dev = MEM // n
+    mine = lambda t: lax.dynamic_slice_in_dim(t, me * 2, 2, 0)
+    device, slot, count = mine(near_device), mine(near_slot), mine(near_count)
+    named = device[:, :, None] == jnp.arange(n)[None, None, :]
+    alive = jnp.arange(near_width)[None, :] < count[:, None]
+    live = jnp.any(jnp.logical_and(named, alive[:, :, None]), axis=1)
+    bias = jnp.repeat(jnp.where(live, 0.0, -jnp.inf).astype(F32), BLK, axis=1)
+    picked = jnp.sum(jnp.where(named, slot[:, :, None], 0), axis=(0, 1)).astype(F32)
+    picked = jnp.broadcast_to(picked[:, None], (n, HD))
+    second = (writer_block % 2).astype(F32).reshape(MEM, 1)
+    pack = 2 * tokens + rows_dev
+    dma = pltpu.SemaphoreType.DMA
+    vmem = pl.BlockSpec(memory_space=pltpu.VMEM)
+    outs = pl.pallas_call(
+        functools.partial(fused_kernel, lines, peers),
+        out_shape=[jax.ShapeDtypeStruct((tokens, width), BF16)] * 4
+        + [jax.ShapeDtypeStruct((rows_dev, width), F32)],
+        in_specs=[vmem] * 8,
+        out_specs=[vmem] * 5,
+        scratch_shapes=[
+            pltpu.VMEM((HEADS, n, 2 * tokens, HD), BF16),
+            pltpu.VMEM((HEADS, 2, lines, pack, HD), BF16),
+            pltpu.VMEM((HEADS, lines, pack, HD), BF16),
+            pltpu.VMEM((HEADS, lines, pack, HD), BF16),
+            pltpu.VMEM((HEADS, lines, pack, HD), BF16),
+            pltpu.VMEM((HEADS, rows_dev, HD), BF16),
+            pltpu.VMEM((HEADS, peers - 1, rows_dev, HD), BF16),
+            dma((HEADS, lines)),
+            dma((HEADS, lines)),
+            dma((HEADS, lines)),
+            dma((HEADS, n)),
+            dma((HEADS,)),
+            dma((HEADS,)),
+            dma((HEADS, lines)),
+            dma((HEADS, lines)),
+            dma((HEADS, lines)),
+            dma((HEADS, lines)),
+            dma((HEADS, peers - 1)),
+            dma((HEADS, peers - 1)),
+        ],
+        compiler_params=pltpu.CompilerParams(
+            collective_id=0, has_side_effects=True, vmem_limit_bytes=60 * 1024 * 1024
+        ),
+    )(
+        queries[0],
+        key_states[0],
+        value_states[0],
+        out_grad[0],
+        memory,
+        second,
+        bias,
+        picked,
+    )
+    return tuple(o[None] for o in outs[:4]) + (outs[4],)
+
+
 def solution(mesh):
     placed = (P("batch", "seq", None),) * 4 + (P(),) * 5
+    one_line = mesh.shape["seq"] == 8 and mesh.shape["batch"] == 4
     return jax.shard_map(
-        shards,
+        fused if one_line else shards,
         mesh=mesh,
         in_specs=placed,
         out_specs=(P("batch", "seq", None),) * 4 + (P("seq", None),),

time: 283 us -> 162 us (0.57)
  waiting for transfers between devices: 227 us -> 0 us
  Pallas kernels: 27.6 us -> 148 us
  between operations: 13.9 us -> 0.67 us
  other arithmetic: 7.63 us -> 0.96 us
  local copies, waits for them, and re-layouts: 5.9 us -> 12.4 us
    pallas_call x2 -> x1, Pallas kernels: 27.6 us -> 148 us  [fused(): pl.pallas_call(functools.partial(fused_kernel, lines, peers), out_shape=[...]
    reduce_scatter x2 -> x0, waiting for transfers between devices: 105 us -> none  [shards(): got = lax.psum_scatter(out, 'seq', scatter_dimension=0, tiled=False)]
    all_gather x2 -> x0, waiting for transfers between devices: 83.3 us -> none  [shards(): gathered.append(lax.all_gather(packed, 'seq', axis=0, tiled=False))]
    psum x1 -> x0, waiting for transfers between devices: 39.1 us -> none  [shards(): memory_grad = lax.psum(rows, 'batch').astype(F32)]
    unnamed x14 -> x9, local copies, waits for them, and re-layouts: 0.21 us -> 9 us
    slice x5 -> x0, local copies, waits for them, and re-layouts: 5.31 us -> none  [the longest x2 2.13 us: shards(): got[tokens:2 * tokens]]
    broadcast_in_dim x4 -> x0, other arithmetic: 3.44 us -> none  [shards(): return (att[None], qg[None], kg[None], vg[None], memory_grad)]
  transfers between devices with their start and end apart: 5 -> 0, of which waited for: 5 -> 0; matrix products, arithmetic and copies ran while one was open for 3% -> 0% of each run, Pallas kernels for 10% -> 0%
where the time goes in v2:
time: 162 us
  Pallas kernels  148 us (91%)
  local copies, waits for them, and re-layouts  12.4 us (8%)
    pallas_call x1, Pallas kernels, fused(): pl.pallas_call(functools.partial(fused_kernel, lines, peers), out_shape=[...  148 us
    unnamed x9, local copies, waits for them, and re-layouts  9 us

profile of v2, /device:TPU:0, one launch (start us, length us, event | category | flops | bytes accessed | tf_op | source)
XLA Modules:
  0.0 161.9 jit_solution(18405370503905897005)
XLA Ops:
  0.6 0.7 dynamic_slice.10
  1.4 0.1 iota_compare_fusion.1
  1.4 0.8 constant_dynamic-slice_fusion
  2.2 0.1 copy.20
  2.3 0.1 copy.19
  2.4 0.1 select_reduce_fusion
  2.5 0.1 fusion.3
  2.6 0.7 broadcast_in_dim.52.slot_ref
  3.3 0.7 fusion.1
  4.0 0.1 broadcast_bitcast_fusion
  4.0 0.6 copy.24
  4.6 1.0 copy.21.second_ref
  5.7 147.9 %shard_map.128 = (bf16[256,1024]{1,0:T(8,128)(2,1)}, bf16[256,1024]{1,0:T(8,128)(2,1)}, bf16[256,1024]{1,0:T(8,128)(2,1)}, bf16[256,1024]{1,0:T(8,128)(2,1)}, f32[128,1024]{1,0:T(8,128)}) custom-call(bf16[256,1024]{1,0:T(8,128)(2,1)} %bitcast.14, bf16[256,1024]{1,0:T(8,128)(2,1)} %bitcast.15, bf16[256,1024]{1,0:T(8,128)(2,1)} %bitcast.16, ...), custom_call_target="tpu_custom_call" | custom-call | tf_op jit(solution)/shard_map/pallas_call | solution.py:593
  153.5 0.0 copy-start
  153.5 1.9 %copy.30 = bf16[1,256,1024]{2,1,0:T(8,128)(2,1)} copy(bf16[1,256,1024]{2,1,0:T(8,128)(2,1)} %bitcast.21) | data formatting | bytes 1048576
  155.5 1.9 %copy.31 = bf16[1,256,1024]{2,1,0:T(8,128)(2,1)} copy(bf16[1,256,1024]{2,1,0:T(8,128)(2,1)} %bitcast.20) | data formatting | bytes 1048576
  157.3 1.9 %copy.32 = bf16[1,256,1024]{2,1,0:T(8,128)(2,1)} copy(bf16[1,256,1024]{2,1,0:T(8,128)(2,1)} %bitcast.19) | data formatting | bytes 1048576
  159.2 1.9 %copy.33 = bf16[1,256,1024]{2,1,0:T(8,128)(2,1)} copy(bf16[1,256,1024]{2,1,0:T(8,128)(2,1)} %bitcast.18) | data formatting | bytes 1048576
  161.1 0.0 copy-done
  161.1 0.8 copy.34
  (2 shorter events, 0.0 us)
Async XLA Ops:
  153.5 7.5 %copy-start = (f32[128,1024]{1,0:T(8,128)S(1)}, f32[128,1024]{1,0:T(8,128)}, u32[]{:S(2)}) copy-start(f32[128,1024]{1,0:T(8,128)} %get-tuple-element.26) | copy-start | bytes 1572868

commit v3 on v2

--- a/solution.py
+++ b/solution.py
@@ -210,7 +210,7 @@
     v_ref,
     g_ref,
     mem_ref,
-    second_ref,
+    writer_ref,
     bias_ref,
     slot_ref,
     att_ref,
@@ -223,6 +223,10 @@
     sib,
     ups,
     downs,
+    acc,
+    tsum,
+    tgot,
+    second_mask,
     rows_own,
     rows_got,
     up_send,
@@ -235,6 +239,8 @@
     ups_recv,
     downs_send,
     downs_recv,
+    tsum_send,
+    tsum_recv,
     rows_send,
     rows_recv,
 ):
@@ -248,6 +254,7 @@
     b = lax.axis_index("batch")
     z, core = me // 2, me % 2
     last = lines - 1
+    quarter = rows_dev // peers
 
     def at(zz, cc):
         return (b, zz * 2 + cc)
@@ -306,7 +313,7 @@
 
     def sum_up(h, d):
         return send(
-            own.at[h, core, d],
+            acc.at[h, d],
             ups.at[h, d],
             ups_send.at[h, d],
             ups_recv.at[h, d],
@@ -315,7 +322,7 @@
 
     def sum_down(h, d):
         return send(
-            own.at[h, core, d],
+            acc.at[h, d],
             downs.at[h, d],
             downs_send.at[h, d],
             downs_recv.at[h, d],
@@ -331,6 +338,23 @@
             ((b + p + 1) % peers, me),
         )
 
+    def part(p):
+        return pl.ds(pl.multiple_of(p * quarter, quarter), quarter)
+
+    def tsum_copy(h, p):
+        peer = (b + p + 1) % peers
+        return send(
+            tsum.at[h, :, part(peer), :],
+            tgot.at[h, p],
+            tsum_send.at[h, p],
+            tsum_recv.at[h, p],
+            (peer, me),
+        )
+
+    for d in range(n):
+        odd = (writer_ref[d : d + 1, :] % 2).astype(F32)
+        second_mask[d] = jnp.broadcast_to(odd, (rows_dev, HD)).T
+
     def lanes(h):
         return pl.ds(pl.multiple_of(h * HD, HD), HD)
 
@@ -376,7 +400,7 @@
         g = g_ref[:, lanes(h)]
         values = kv[h, :, tokens:, :].astype(F32).reshape(n, 2, BLK, HD)
         sums = jnp.sum(values, axis=2)
-        second = second_ref[...].reshape(n, rows_dev, 1) > 0.5
+        second = second_mask[...] > 0.5
         add = jnp.where(second, sums[:, 1:2, :], sums[:, 0:1, :])
         mem_keys = (mem_ref[:, lanes(h)].reshape(n, rows_dev, HD) + add * block_scale).astype(BF16)
         mem_keys = mem_keys.reshape(MEM, HD)
@@ -410,13 +434,14 @@
         w_mem = p_mem.astype(BF16)
         w_near = p_near.astype(BF16)
         att = (dot_nn(w_mem, mem_keys) + dot_nn(w_near, near_vals)).astype(BF16)
+        att = att.astype(F32)
         att_ref[:, lanes(h)] = att
-        gdot = jnp.sum(g.astype(F32) * att.astype(F32), axis=1, keepdims=True)
+        gdot = jnp.sum(g.astype(F32) * att, axis=1, keepdims=True)
         ds_mem = (p_mem * (dot_nt(g, mem_keys) - gdot)).astype(BF16)
         ds_near = (p_near * (dot_nt(g, near_vals) - gdot)).astype(BF16)
         qg_ref[:, lanes(h)] = (
-            (dot_nn(ds_mem, mem_keys) + dot_nn(ds_near, near_keys)) * scale
-        ).astype(BF16)
+            dot_nn(ds_mem, mem_keys) + dot_nn(ds_near, near_keys)
+        ) * scale
         rows3 = (dot_tn(ds_mem, q) * scale + dot_tn(w_mem, g)).reshape(n, rows_dev, HD)
         first_sum = jnp.sum(jnp.where(second, 0.0, rows3), axis=1, keepdims=True) * block_scale
         second_sum = jnp.sum(jnp.where(second, rows3, 0.0), axis=1, keepdims=True) * block_scale
@@ -444,7 +469,7 @@
     def send_up(h, zz):
         @pl.when(z == zz)
         def _():
-            for d in range(zz + 1, lines):
+            for d in reversed(range(zz + 1, lines)):
                 sum_up(h, d).start()
 
     def send_down(h, zz):
@@ -455,28 +480,39 @@
 
     def sum_first(h):
         sib_copy(h).wait_recv()
-        own[h, core] = plus(own[h, core], sib[h]).astype(BF16)
+        both = 2 * tokens
+        acc[h, :, 0:both, :] = plus(own[h, core, :, 0:both, :], sib[h, :, 0:both, :]).astype(BF16)
+        tsum[h] = plus(own[h, core, :, both:, :], sib[h, :, both:, :]).astype(BF16)
+        for p in range(peers - 1):
+            tsum_copy(h, p).start()
+
+    def sum_rows(h):
+        total = tsum[h, :, part(b), :].astype(F32)
+        for p in range(peers - 1):
+            tsum_copy(h, p).wait_recv()
+            total = total + tgot[h, p].astype(F32)
+        acc[h, :, 2 * tokens :, :] = total.astype(BF16)
         send_up(h, 0)
         send_down(h, last)
 
     def sum_next(h, k):
         @pl.when(z == k)
         def _():
-            for d in range(k + 1, lines):
+            for d in reversed(range(k + 1, lines)):
                 sum_up(h, d).wait_recv()
-                own[h, core, d] = plus(own[h, core, d], ups[h, d]).astype(BF16)
+                acc[h, d] = plus(acc[h, d], ups[h, d]).astype(BF16)
                 sum_up(h, d).start()
 
         @pl.when(z == last - k)
         def _():
             for d in range(last - k):
                 sum_down(h, d).wait_recv()
-                own[h, core, d] = plus(own[h, core, d], downs[h, d]).astype(BF16)
+                acc[h, d] = plus(acc[h, d], downs[h, d]).astype(BF16)
                 sum_down(h, d).start()
 
     def write_sums(h, total):
-        kg_ref[:, lanes(h)] = total[0:tokens].astype(BF16)
-        vg_ref[:, lanes(h)] = total[tokens : 2 * tokens].astype(BF16)
+        kg_ref[:, lanes(h)] = total[0:tokens]
+        vg_ref[:, lanes(h)] = total[tokens : 2 * tokens]
         rows_own[h] = total[2 * tokens :].astype(BF16)
 
     def finish(h):
@@ -490,35 +526,35 @@
 
         @pl.when(z == 0)
         def _():
-            write_sums(h, plus(own[h, core, 0], downs[h, 0]))
+            write_sums(h, plus(acc[h, 0], downs[h, 0]))
 
         @pl.when(z == last)
         def _():
-            write_sums(h, plus(own[h, core, last], ups[h, last]))
+            write_sums(h, plus(acc[h, last], ups[h, last]))
 
         @pl.when(jnp.logical_and(z > 0, z < last))
         def _():
-            write_sums(h, plus(own[h, core, z], ups[h, z]) + downs[h, z].astype(F32))
+            write_sums(h, plus(acc[h, z], ups[h, z]) + downs[h, z].astype(F32))
 
         for p in range(peers - 1):
             row_copy(h, p).start()
 
     def write_rows(h):
-        total = rows_own[h].astype(F32)
+        mg_ref[part(b), lanes(h)] = rows_own[h].astype(F32)
         for p in range(peers - 1):
             row_copy(h, p).wait_recv()
-            total = total + rows_got[h, p].astype(F32)
-        mg_ref[:, lanes(h)] = total
+            mg_ref[part((b + peers - p - 1) % peers), lanes(h)] = rows_got[h, p].astype(F32)
 
     stages = [(0, gather_first)]
     for k in range(1, lines):
         stages.append((k, functools.partial(gather_next, k=k)))
+    stages.append((lines, compute))
     stages.append((lines + 1, sum_first))
+    stages.append((lines + 2, sum_rows))
     for k in range(1, last):
-        stages.append((lines + 1 + k, functools.partial(sum_next, k=k)))
-    stages.append((2 * lines, finish))
-    stages.append((2 * lines + 1, write_rows))
-    stages.append((lines, compute))
+        stages.append((lines + 2 + k, functools.partial(sum_next, k=k)))
+    stages.append((2 * lines + 1, finish))
+    stages.append((2 * lines + 2, write_rows))
 
     def tick(t, carry):
         for lag, stage in stages:
@@ -554,6 +590,7 @@
         sib_copy(h).wait_send()
         for p in range(peers - 1):
             row_copy(h, p).wait_send()
+            tsum_copy(h, p).wait_send()
         return carry
 
     lax.fori_loop(0, HEADS, drain, 0)
@@ -586,13 +623,14 @@
     bias = jnp.repeat(jnp.where(live, 0.0, -jnp.inf).astype(F32), BLK, axis=1)
     picked = jnp.sum(jnp.where(named, slot[:, :, None], 0), axis=(0, 1)).astype(F32)
     picked = jnp.broadcast_to(picked[:, None], (n, HD))
-    second = (writer_block % 2).astype(F32).reshape(MEM, 1)
+    quarter = rows_dev // peers
+    line = 2 * tokens + quarter
     pack = 2 * tokens + rows_dev
     dma = pltpu.SemaphoreType.DMA
     vmem = pl.BlockSpec(memory_space=pltpu.VMEM)
     outs = pl.pallas_call(
         functools.partial(fused_kernel, lines, peers),
-        out_shape=[jax.ShapeDtypeStruct((tokens, width), BF16)] * 4
+        out_shape=[jax.ShapeDtypeStruct((tokens, width), F32)] * 4
         + [jax.ShapeDtypeStruct((rows_dev, width), F32)],
         in_specs=[vmem] * 8,
         out_specs=[vmem] * 5,
@@ -600,10 +638,14 @@
             pltpu.VMEM((HEADS, n, 2 * tokens, HD), BF16),
             pltpu.VMEM((HEADS, 2, lines, pack, HD), BF16),
             pltpu.VMEM((HEADS, lines, pack, HD), BF16),
-            pltpu.VMEM((HEADS, lines, pack, HD), BF16),
-            pltpu.VMEM((HEADS, lines, pack, HD), BF16),
-            pltpu.VMEM((HEADS, rows_dev, HD), BF16),
-            pltpu.VMEM((HEADS, peers - 1, rows_dev, HD), BF16),
+            pltpu.VMEM((HEADS, lines, line, HD), BF16),
+            pltpu.VMEM((HEADS, lines, line, HD), BF16),
+            pltpu.VMEM((HEADS, lines, line, HD), BF16),
+            pltpu.VMEM((HEADS, lines, rows_dev, HD), BF16),
+            pltpu.VMEM((HEADS, peers - 1, lines, quarter, HD), BF16),
+            pltpu.VMEM((n, rows_dev, HD), F32),
+            pltpu.VMEM((HEADS, quarter, HD), BF16),
+            pltpu.VMEM((HEADS, peers - 1, quarter, HD), BF16),
             dma((HEADS, lines)),
             dma((HEADS, lines)),
             dma((HEADS, lines)),
@@ -616,6 +658,8 @@
             dma((HEADS, lines)),
             dma((HEADS, peers - 1)),
             dma((HEADS, peers - 1)),
+            dma((HEADS, peers - 1)),
+            dma((HEADS, peers - 1)),
         ],
         compiler_params=pltpu.CompilerParams(
             collective_id=0, has_side_effects=True, vmem_limit_bytes=60 * 1024 * 1024
@@ -626,11 +670,11 @@
         value_states[0],
         out_grad[0],
         memory,
-        second,
+        writer_block.reshape(n, rows_dev),
         bias,
         picked,
     )
-    return tuple(o[None] for o in outs[:4]) + (outs[4],)
+    return tuple(o.astype(BF16)[None] for o in outs[:4]) + (outs[4],)
 
 
 def solution(mesh):

time: 162 us -> 156 us (0.963)
  local copies, waits for them, and re-layouts: 12.4 us -> 3.83 us
  other arithmetic: 0.96 us -> 7.53 us
  Pallas kernels: 148 us -> 144 us
    unnamed x9 -> x7, local copies, waits for them, and re-layouts: 9 us -> 1.48 us
    broadcast_in_dim x0 -> x4, other arithmetic: none -> 7.27 us  [fused(): return tuple((o.astype(BF16)[None] for o in outs[:4])) + (outs[4],)]
    pallas_call x1, Pallas kernels: 148 us -> 144 us  [fused(): pl.pallas_call(functools.partial(fused_kernel, lines, peers), out_shape=[...]
where the time goes in v3:
time: 156 us
  Pallas kernels  144 us (92%)
  other arithmetic  7.53 us (5%)
  local copies, waits for them, and re-layouts  3.83 us (2%)
    pallas_call x1, Pallas kernels, fused(): pl.pallas_call(functools.partial(fused_kernel, lines, peers), out_shape=[...  144 us
    broadcast_in_dim x4, other arithmetic, fused(): return tuple((o.astype(BF16)[None] for o in outs[:4])) + (outs[4],)  7.27 us

profile of v3, /device:TPU:0, one launch (start us, length us, event | category | flops | bytes accessed | tf_op | source)
XLA Modules:
  0.0 156.0 jit_solution(13253802550525516861)
XLA Ops:
  0.6 0.7 dynamic_slice.10
  1.4 0.1 iota_compare_fusion.1
  1.4 0.8 constant_dynamic-slice_fusion
  2.2 0.1 copy.17
  2.3 0.1 copy.16
  2.4 0.1 select_reduce_fusion
  2.5 0.1 fusion.1
  2.6 0.7 broadcast_in_dim.52.slot_ref
  3.3 0.1 broadcast_bitcast_fusion
  3.3 0.6 copy.20
  3.9 144.0 %shard_map.128 = (f32[256,1024]{1,0:T(8,128)}, f32[256,1024]{1,0:T(8,128)}, f32[256,1024]{1,0:T(8,128)}, f32[256,1024]{1,0:T(8,128)}, f32[128,1024]{1,0:T(8,128)}) custom-call(bf16[256,1024]{1,0:T(8,128)(2,1)} %bitcast.18, bf16[256,1024]{1,0:T(8,128)(2,1)} %bitcast.19, bf16[256,1024]{1,0:T(8,128)(2,1)} %bitcast.20, bf16[256,1024]{1,0:T(8,128)(2,1)} %bitcast.21, ...), custom_call_target="tpu_custom_call" | custom-call | tf_op jit(solution)/shard_map/pallas_call | solution.py:631
  148.0 0.0 copy-start
  148.0 0.0 copy-start.1
  148.0 2.2 %convert_bitcast_fusion.3 = bf16[1,256,1024]{2,1,0:T(8,128)(2,1)} fusion(f32[256,1024]{1,0:T(8,128)} %get-tuple-element.10), kind=kLoop, calls=%fused_computation.3 | loop fusion | flops 262144 | bytes 1572864 | tf_op jit(solution)/shard_map/broadcast_in_dim | solution.py:677
  150.2 2.1 %convert_bitcast_fusion.2 = bf16[1,256,1024]{2,1,0:T(8,128)(2,1)} fusion(f32[256,1024]{1,0:T(8,128)} %get-tuple-element.11), kind=kLoop, calls=%fused_computation.2 | loop fusion | flops 262144 | bytes 1572864 | tf_op jit(solution)/shard_map/broadcast_in_dim | solution.py:677
  152.3 2.1 %convert_bitcast_fusion.1 = bf16[1,256,1024]{2,1,0:T(8,128)(2,1)} fusion(f32[256,1024]{1,0:T(8,128)} %get-tuple-element.12), kind=kLoop, calls=%fused_computation.1 | loop fusion | flops 262144 | bytes 1572864 | tf_op jit(solution)/shard_map/broadcast_in_dim | solution.py:677
  154.4 0.0 copy-done
  154.4 0.9 convert_bitcast_fusion
  155.2 0.0 copy-done.1
  155.3 0.8 copy.22
  (2 shorter events, 0.0 us)
Async XLA Ops:
  148.0 6.4 %copy-start = (f32[256,1024]{1,0:T(8,128)S(1)}, f32[256,1024]{1,0:T(8,128)}, u32[]{:S(2)}) copy-start(f32[256,1024]{1,0:T(8,128)} %get-tuple-element.13) | copy-start | bytes 3145732
  148.0 7.3 %copy-start.1 = (f32[128,1024]{1,0:T(8,128)S(1)}, f32[128,1024]{1,0:T(8,128)}, u32[]{:S(2)}) copy-start(f32[128,1024]{1,0:T(8,128)} %get-tuple-element.26) | copy-start | bytes 1572868

commit v4 on v3

--- a/solution.py
+++ b/solution.py
@@ -358,16 +358,23 @@
     def lanes(h):
         return pl.ds(pl.multiple_of(h * HD, HD), HD)
 
+    def gather_ends(t):
+        for h in (2 * t, 2 * t + 1):
+            kv[h, me, 0:tokens, :] = k_ref[:, lanes(h)]
+            kv[h, me, tokens : 2 * tokens, :] = v_ref[:, lanes(h)]
+
+            @pl.when(z == 0)
+            def _(h=h):
+                kv_up(h, 0).start()
+
+            @pl.when(z == last)
+            def _(h=h):
+                kv_down(h, last).start()
+
     def gather_first(h):
-        kv[h, me, 0:tokens, :] = k_ref[:, lanes(h)]
-        kv[h, me, tokens : 2 * tokens, :] = v_ref[:, lanes(h)]
-
-        @pl.when(z < last)
+        @pl.when(jnp.logical_and(z > 0, z < last))
         def _():
             kv_up(h, z).start()
-
-        @pl.when(z > 0)
-        def _():
             kv_down(h, z).start()
 
         kv_share(h, z).start()
@@ -557,6 +564,10 @@
     stages.append((2 * lines + 2, write_rows))
 
     def tick(t, carry):
+        @pl.when(t < HEADS // 2)
+        def _():
+            gather_ends(t)
+
         for lag, stage in stages:
 
             @pl.when(jnp.logical_and(t >= lag, t < HEADS + lag))

time: 156 us -> 153 us (0.981)
  Pallas kernels: 144 us -> 140 us
    pallas_call x1, Pallas kernels: 144 us -> 140 us  [fused(): pl.pallas_call(functools.partial(fused_kernel, lines, peers), out_shape=[...]
where the time goes in v4:
time: 153 us; the launch traced here: 152 us
  Pallas kernels  140 us (92%)
  other arithmetic  7.53 us (5%)
  local copies, waits for them, and re-layouts  3.83 us (3%)
    pallas_call x1, Pallas kernels, fused(): pl.pallas_call(functools.partial(fused_kernel, lines, peers), out_shape=[...  140 us
    broadcast_in_dim x4, other arithmetic, fused(): return tuple((o.astype(BF16)[None] for o in outs[:4])) + (outs[4],)  7.27 us

profile of v4, /device:TPU:0, one launch (start us, length us, event | category | flops | bytes accessed | tf_op | source)
XLA Modules:
  0.0 152.4 jit_solution(16941324715464312309)
XLA Ops:
  0.6 0.7 dynamic_slice.10
  1.4 0.1 iota_compare_fusion.1
  1.4 0.8 constant_dynamic-slice_fusion
  2.2 0.1 copy.17
  2.3 0.1 copy.16
  2.4 0.1 select_reduce_fusion
  2.5 0.1 fusion.1
  2.6 0.7 broadcast_in_dim.52.slot_ref
  3.3 0.1 broadcast_bitcast_fusion
  3.3 0.6 copy.20
  3.9 140.3 %shard_map.128 = (f32[256,1024]{1,0:T(8,128)}, f32[256,1024]{1,0:T(8,128)}, f32[256,1024]{1,0:T(8,128)}, f32[256,1024]{1,0:T(8,128)}, f32[128,1024]{1,0:T(8,128)}) custom-call(bf16[256,1024]{1,0:T(8,128)(2,1)} %bitcast.18, bf16[256,1024]{1,0:T(8,128)(2,1)} %bitcast.19, bf16[256,1024]{1,0:T(8,128)(2,1)} %bitcast.20, bf16[256,1024]{1,0:T(8,128)(2,1)} %bitcast.21, ...), custom_call_target="tpu_custom_call" | custom-call | tf_op jit(solution)/shard_map/pallas_call | solution.py:642
  144.3 0.0 copy-start
  144.3 0.0 copy-start.1
  144.3 2.2 %convert_bitcast_fusion.3 = bf16[1,256,1024]{2,1,0:T(8,128)(2,1)} fusion(f32[256,1024]{1,0:T(8,128)} %get-tuple-element.10), kind=kLoop, calls=%fused_computation.3 | loop fusion | flops 262144 | bytes 1572864 | tf_op jit(solution)/shard_map/broadcast_in_dim | solution.py:688
  146.5 2.1 %convert_bitcast_fusion.2 = bf16[1,256,1024]{2,1,0:T(8,128)(2,1)} fusion(f32[256,1024]{1,0:T(8,128)} %get-tuple-element.11), kind=kLoop, calls=%fused_computation.2 | loop fusion | flops 262144 | bytes 1572864 | tf_op jit(solution)/shard_map/broadcast_in_dim | solution.py:688
  148.6 2.1 %convert_bitcast_fusion.1 = bf16[1,256,1024]{2,1,0:T(8,128)(2,1)} fusion(f32[256,1024]{1,0:T(8,128)} %get-tuple-element.12), kind=kLoop, calls=%fused_computation.1 | loop fusion | flops 262144 | bytes 1572864 | tf_op jit(solution)/shard_map/broadcast_in_dim | solution.py:688
  150.7 0.0 copy-done
  150.7 0.9 convert_bitcast_fusion
  151.6 0.0 copy-done.1
  151.6 0.8 copy.22
  (2 shorter events, 0.0 us)
Async XLA Ops:
  144.3 6.4 %copy-start = (f32[256,1024]{1,0:T(8,128)S(1)}, f32[256,1024]{1,0:T(8,128)}, u32[]{:S(2)}) copy-start(f32[256,1024]{1,0:T(8,128)} %get-tuple-element.13) | copy-start | bytes 3145732
  144.3 7.3 %copy-start.1 = (f32[128,1024]{1,0:T(8,128)S(1)}, f32[128,1024]{1,0:T(8,128)}, u32[]{:S(2)}) copy-start(f32[128,1024]{1,0:T(8,128)} %get-tuple-element.26) | copy-start | bytes 1572868
